TPU v7x, 128 devices: a whole 4x4x4 slice. The times are simulated.
128 devices in a mesh: expert: 4 (over y), feat: 32 (over x, z, core).
Axes of the slice: x: 4, y: 4, z: 4, core: 2. Of those that a mesh axis runs over, the one named last changes fastest.
Arguments:
- tokens: bfloat16 [1024, 4096], P(('expert', 'feat')), may hold values from -6 to 6
- expert_ids: int32 [1024, 2], P(('expert', 'feat')), may hold values from 0 to 7, as said below
- route_weights: bfloat16 [1024, 2], P(('expert', 'feat')), may hold values from 0.099609375 to 1
- gate_proj: bfloat16 [4096, 28672], P(None, ('expert', 'feat')), may hold values from -0.09375 to 0.09375
- up_proj: bfloat16 [4096, 28672], P(None, ('expert', 'feat')), may hold values from -0.09375 to 0.09375
- down_proj: bfloat16 [28672, 4096], P(('expert', 'feat')), may hold values from -0.046875 to 0.046875
- enc_weight: float32 [4096, 32768], P(None, ('expert', 'feat')), may hold values from -0.09375 to 0.09375
- enc_bias: float32 [32768], P(('expert', 'feat')), may hold values from -3 to 3
- log_threshold: float32 [32768], P(('expert', 'feat')), may hold values from -2.3 to 0
- dec_weight: float32 [32768, 4096], P(('expert', 'feat')), may hold values from -0.046875 to 0.046875
Outputs:
- grad_encoder: float32 [4096, 32768], P(None, ('expert', 'feat'))
- grad_decoder: float32 [32768, 4096], P(('expert', 'feat'))
- grad_bias: float32 [32768], P(('expert', 'feat'))
- grad_threshold: float32 [32768], P(('expert', 'feat'))
Inputs may be any that keep to these rules, and one draw needn't show every extreme that they name: `expert_ids`: each token names two different experts of 0 to 7. Among the 8 tokens of one device, each expert below 2 is named by at most 4 tokens; in every draw one of these experts, drawn from the seed and the same for all devices, is named by exactly 4 tokens of every device.
All inputs are finite; a program needn't handle non-finite values.
Results may differ from a plain program's by a relative error of at most 0.0021.
Values may be sent and summed in bfloat16 or wider, within the bound.
A program may use at most 128 MiB of HBM per device.

v0:
```python
import jax
import jax.numpy as jnp
from jax import lax
from jax.sharding import PartitionSpec as P

sharpness = 0.1
kernel_width = 0.5
density_weight = 0.01


def partner(block, axis, stride):
    count = lax.axis_size(axis)
    route = []
    for low in range(count):
        high = low | 1 << stride
        if high != low and high < count:
            route += [(low, high), (high, low)]
    return lax.ppermute(block, axis, route)


def pack_slots(tokens, expert_ids, route_weights, experts):
    capacity = tokens.shape[0] // 2
    window = jnp.arange(experts, dtype=jnp.int32)
    matches = expert_ids[:, :, None] == window[None, None, :]
    named = jnp.sum(matches.astype(jnp.int32), axis=1)
    weighted = jnp.sum(
        jnp.where(matches, route_weights[:, :, None], jnp.zeros((), jnp.bfloat16)), axis=1
    )
    rows = jnp.arange(tokens.shape[0], dtype=jnp.int32)
    earlier = rows[None, :, None] < rows[:, None, None]
    slot_index = jnp.sum(jnp.where(earlier, named[None, :, :], 0), axis=1)
    places = jnp.arange(capacity, dtype=jnp.int32)
    chosen = (named.T[:, None, :] == 1) & (slot_index.T[:, None, :] == places[None, :, None])
    slot_rows = jnp.einsum(
        "ect,td->ecd", chosen.astype(jnp.bfloat16), tokens, preferred_element_type=jnp.float32
    ).astype(jnp.bfloat16)
    slot_weights = jnp.sum(
        jnp.where(chosen, weighted.T[:, None, :], jnp.zeros((), jnp.bfloat16)), axis=2
    )
    return (slot_rows, slot_weights)


def split(value):
    high = lax.reduce_precision(value, 8, 7)
    return (high.astype(jnp.bfloat16), (value - high).astype(jnp.bfloat16))


def product(left, right, dims):
    return lax.dot_general(left, right, (dims, ((), ())), preferred_element_type=jnp.float32)


def body(
    tokens,
    expert_ids,
    route_weights,
    gate_proj,
    up_proj,
    down_proj,
    enc_weight,
    enc_bias,
    log_threshold,
    dec_weight,
):
    copies = 2
    experts = lax.axis_size("expert") // copies
    slot_rows, slot_weights = pack_slots(tokens, expert_ids, route_weights, experts)
    send_rows = jnp.repeat(slot_rows, copies, axis=0)
    send_weights = jnp.repeat(slot_weights, copies, axis=0)
    came_rows, came_weights = (
        lax.all_to_all(send_rows, "expert", split_axis=0, concat_axis=0, tiled=True),
        lax.all_to_all(send_weights, "expert", split_axis=0, concat_axis=0, tiled=True),
    )
    all_rows, all_weights = (
        lax.all_gather(came_rows, "feat", axis=0, tiled=True),
        lax.all_gather(came_weights, "feat", axis=0, tiled=True),
    )
    width = tokens.shape[1]
    token_rows = all_rows.reshape(-1, width)
    row_weights = all_weights.reshape(-1).astype(jnp.float32)
    gate_act = jnp.dot(token_rows, gate_proj, preferred_element_type=jnp.float32)
    up_act = jnp.dot(token_rows, up_proj, preferred_element_type=jnp.float32)
    hidden = (jax.nn.silu(gate_act) * up_act).astype(jnp.bfloat16)
    target_part = jnp.dot(hidden, down_proj, preferred_element_type=jnp.float32)
    rows = ((1,), (0,))
    down = ((0,), (0,))
    enc_high, enc_low = split(enc_weight)
    dec_high, dec_low = split(dec_weight)
    preact = product(token_rows, enc_high, rows) + product(token_rows, enc_low, rows) + enc_bias
    threshold = jnp.exp(log_threshold)
    shifted = preact - threshold
    soft_gate = jax.nn.sigmoid(shifted / sharpness)
    active = preact * soft_gate
    act_high, act_low = split(active)
    recon = product(act_high, dec_high, rows) + product(act_high, dec_low, rows)
    partial_error = recon + product(act_low, dec_high, rows) - target_part
    feat_total = lax.psum_scatter(partial_error, "feat", scatter_dimension=0, tiled=True)
    recon_error = feat_total + partner(feat_total, "expert", 0)
    own_rows = feat_total.shape[0]
    own_weights = lax.dynamic_slice_in_dim(row_weights, lax.axis_index("feat") * own_rows, own_rows)
    own_grad = (2.0 * own_weights[:, None] * recon_error).astype(jnp.bfloat16)
    residual_grad = lax.all_gather(own_grad, "feat", axis=0, tiled=True)
    grad_decoder = product(act_high, residual_grad, down) + product(act_low, residual_grad, down)
    across = ((1,), (1,))
    grad_active = product(residual_grad, dec_high, across) + product(residual_grad, dec_low, across)
    grad_pre = grad_active * soft_gate
    pre_high, pre_low = split(grad_pre)
    grad_encoder = product(token_rows, pre_high, down) + product(token_rows, pre_low, down)
    grad_bias = jnp.sum(grad_pre, axis=0)
    kernel = jnp.maximum(0.0, 1.0 - jnp.abs(shifted) / kernel_width) / kernel_width
    slope_sum = jnp.sum(
        (grad_active * threshold + density_weight * row_weights[:, None]) * kernel, axis=0
    )
    grad_threshold = -threshold * slope_sum
    return (grad_encoder, grad_decoder, grad_bias, grad_threshold)


def solution(mesh):
    in_specs = (
        P(("expert", "feat"), None),
        P(("expert", "feat"), None),
        P(("expert", "feat"), None),
        P(None, ("expert", "feat")),
        P(None, ("expert", "feat")),
        P(("expert", "feat"), None),
        P(None, ("expert", "feat")),
        P(("expert", "feat")),
        P(("expert", "feat")),
        P(("expert", "feat"), None),
    )
    out_specs = (
        P(None, ("expert", "feat")),
        P(("expert", "feat"), None),
        P(("expert", "feat")),
        P(("expert", "feat")),
    )
    return jax.shard_map(body, mesh=mesh, in_specs=in_specs, out_specs=out_specs, check_vma=False)
```

profile of v0, /device:TPU:1, one launch (start us, length us, event | category | flops | bytes accessed | tf_op | source)
XLA Modules:
  0.0 313.5 jit_solution(17543353753348144969)
XLA Ops:
  7.2 0.8 convert_reduce_fusion.1
  8.2 1.0 convolution_convert_fusion
  9.3 9.7 %all_to_all.17 = bf16[4,4,4096]{2,1,0:T(4,128)(2,1)} all-to-all(bf16[4,4,4096]{2,1,0:T(4,128)(2,1)S(1)} %bitcast.22), channel_id=1, replica_groups=mesh['expert'=4,'feat'=32] {'expert'}, dimensions={0} | all-to-all | bytes 262144 | tf_op jit(solution)/shard_map/all_to_all | solution.py:70
  19.1 0.7 exp.10
  19.8 48.0 %all-gather.4.cloned.1.call-done = bf16[128,4,4096]{2,1,0:T(4,128)(2,1)} async-done(((bf16[4,4,4096]{2,1,0:T(4,128)(2,1)}), bf16[128,4,4096]{2,1,0:T(4,128)(2,1)}) %all-gather.4.cloned.1.call-update) | async-done | bytes 4194320 | tf_op jit(solution)/shard_map/all_gather | solution.py:74
  67.8 6.9 %reshape.55 = bf16[512,4096]{1,0:T(8,128)(2,1)} reshape(bf16[128,4,4096]{2,1,0:T(4,128)(2,1)} %all-gather.4.cloned.1.call-done) | data formatting | bytes 8388608 | tf_op jit(solution)/shard_map/reshape | solution.py:78
  74.6 4.9 %fusion.2 = f32[512,256]{1,0:T(8,128)S(1)} fusion(bf16[512,4096]{1,0:T(8,128)(2,1)} %reshape.55, f32[4096,256]{1,0:T(8,128)} %param.16), kind=kOutput, calls=%fused_computation.10 | convolution fusion | flops 1076887552 | bytes 8912896 | tf_op jit(solution)/shard_map/dot_general | solution.py:49
  79.5 1.0 copy-done.7
  80.6 1.3 fusion.6
  81.8 0.9 copy-done.5
  82.8 4.6 %fusion.11 = f32[512,4096]{1,0:T(8,128)} fusion(f32[256,4096]{1,0:T(8,128)S(1)} %copy-done.5, f32[512,256]{1,0:T(8,128)S(1)} %fusion.6, f32[256]{0:T(256)S(1)} %exp.10), kind=kOutput, calls=%fused_computation.23 | convolution fusion | flops 1077936128 | bytes 13108224 | tf_op jit(solution)/shard_map/dot_general | solution.py:49
  87.3 4.5 %fusion.38 = f32[512,4096]{1,0:T(8,128)} fusion(f32[256,4096]{1,0:T(8,128)S(1)} %copy-done.5, f32[512,256]{1,0:T(8,128)S(1)} %fusion.6, f32[256]{0:T(256)S(1)} %exp.10), kind=kOutput, calls=%fused_computation.58 | convolution fusion | flops 1076887552 | bytes 13108224 | tf_op jit(solution)/shard_map/dot_general | solution.py:49
  91.9 1.4 fusion.46
  93.3 8.7 %fusion.8 = f32[512,4096]{1,0:T(8,128)} fusion(bf16[224,4096]{1,0:T(8,128)(2,1)S(1)} %copy-done, bf16[512,4096]{1,0:T(8,128)(2,1)} %reshape.55, bf16[4096,224]{0,1:T(8,128)(2,1)} %param.14, f32[512,224]{0,1:T(8,128)S(1)} %fusion.46), kind=kOutput, calls=%fused_computation.17 | convolution fusion | flops 1879736320 | bytes 16711680 | tf_op jit(solution)/shard_map/dot_general | solution.py:83
  102.0 14.3 %add_subtract_fusion = f32[512,4096]{1,0:T(8,128)} fusion(f32[512,4096]{1,0:T(8,128)} %fusion.8, f32[512,4096]{1,0:T(8,128)} %fusion.38, f32[512,4096]{1,0:T(8,128)} %fusion.11, f32[256,4096]{1,0:T(8,128)} %param.19, f32[512,256]{1,0:T(8,128)S(1)} %fusion.6, f32[256]{0:T(256)S(1)} %exp.10), kind=kOutput, calls=%fused_computation | convolution fusion | flops 1083310080 | bytes 38274048 | tf_op jit(solution)/shard_map/dot_general | solution.py:49
  116.3 0.7 copy-done.10
  117.0 89.5 %reduce-scatter.2.cloned.1.call-done = f32[16,4096]{1,0:T(8,128)} async-done(((f32[512,4096]{1,0:T(8,128)}), f32[16,4096]{1,0:T(8,128)}) %reduce-scatter.2.cloned.1.call-update) | async-done | bytes 262160 | tf_op jit(solution)/shard_map/reduce_scatter | solution.py:96
  206.5 1.2 collective-permute-start
  207.8 0.6 copy.24
  208.4 3.7 %all-to-all-start.1 = ((bf16[4,1,4]{2,1,0:T(2,128)(2,1)}), bf16[4,1,4]{2,1,0:T(2,128)(2,1)S(1)}, u32[]{:S(2)}, u32[]{:S(2)}) async-start(bf16[4,1,4]{2,1,0:T(2,128)(2,1)} %copy.24), calls=%async_computation.1 | async-start | bytes 4096 | tf_op jit(solution)/shard_map/all_to_all | solution.py:71
  212.1 4.1 %all-to-all-done.1 = bf16[4,1,4]{2,1,0:T(2,128)(2,1)S(1)} async-done(((bf16[4,1,4]{2,1,0:T(2,128)(2,1)}), bf16[4,1,4]{2,1,0:T(2,128)(2,1)S(1)}, u32[]{:S(2)}, u32[]{:S(2)}) %all-to-all-start.1) | async-done | bytes 64 | tf_op jit(solution)/shard_map/all_to_all | solution.py:71
  216.2 27.5 %all-gather = bf16[128,1,4]{2,1,0:T(2,128)(2,1)S(1)} all-gather(bf16[4,1,4]{2,1,0:T(2,128)(2,1)S(1)} %all-to-all-done.1), channel_id=2, replica_groups=mesh['expert'=4,'feat'=32] {'feat'}, dimensions={0}, use_global_device_ids=true | all-gather | bytes 1056 | tf_op jit(solution)/shard_map/all_gather | solution.py:75
  244.1 1.7 multiply_convert_fusion
  245.8 43.2 %all-gather.6.cloned.1.call-done = bf16[512,4096]{1,0:T(8,128)(2,1)} async-done(((bf16[16,4096]{1,0:T(8,128)(2,1)}), bf16[512,4096]{1,0:T(8,128)(2,1)}) %all-gather.6.cloned.1.call-update) | async-done | bytes 4194320 | tf_op jit(solution)/shard_map/all_gather | solution.py:101
  289.0 4.9 %fusion.9 = f32[512,256]{1,0:T(8,128)S(1)} fusion(bf16[512,4096]{1,0:T(8,128)(2,1)} %all-gather.6.cloned.1.call-done, f32[256,4096]{1,0:T(8,128)} %param.19), kind=kOutput, calls=%fused_computation.22 | convolution fusion | flops 1076887552 | bytes 8912896 | tf_op jit(solution)/shard_map/dot_general | solution.py:49
  293.9 1.0 copy-done.6
  294.9 2.0 fusion.44
  296.9 0.6 negate_multiply_fusion
  297.5 1.3 fusion.23
  298.8 3.3 %convolution_add_fusion.1 = f32[4096,256]{1,0:T(8,128)} fusion(f32[4096,256]{1,0:T(8,128)S(1)} %fusion.23, bf16[512,4096]{1,0:T(8,128)(2,1)S(1)} %copy-done.3, f32[512,256]{1,0:T(8,128)S(1)} %get-tuple-element.5), kind=kOutput, calls=%fused_computation.6 | convolution fusion | flops 1075183616 | bytes 13107200 | tf_op jit(solution)/shard_map/dot_general | solution.py:49
  302.1 1.4 fusion.25
  303.5 3.5 %convolution_add_fusion = f32[256,4096]{1,0:T(8,128)} fusion(f32[256,4096]{1,0:T(8,128)S(1)} %fusion.25, bf16[512,4096]{1,0:T(8,128)(2,1)S(1)} %copy-done.4, f32[512,256]{1,0:T(8,128)S(1)} %fusion.6, f32[256]{0:T(256)S(1)} %exp.10), kind=kOutput, calls=%fused_computation.5 | convolution fusion | flops 1075838976 | bytes 13108224 | tf_op jit(solution)/shard_map/dot_general | solution.py:49
  (40 shorter events, 0.9 us)
Async XLA Ops:
  7.2 86.1 %copy-start = (bf16[224,4096]{1,0:T(8,128)(2,1)S(1)}, bf16[224,4096]{1,0:T(8,128)(2,1)}, u32[]{:S(2)}) copy-start(bf16[224,4096]{1,0:T(8,128)(2,1)} %param.15) | copy-start | bytes 5505028
  7.2 60.6 %all-gather.4.cloned.1.call-start = ((), (), s32[]{:S(2)}) async-start(), calls=%async_computation.3 | async-start | bytes 4325376 | tf_op jit(solution)/shard_map/all_gather | solution.py:74
  19.0 187.5 %reduce-scatter.2.cloned.1.call-start = ((), (), s32[]{:S(2)}) async-start(), calls=%async_computation.4 | async-start | bytes 8650752 | tf_op jit(solution)/shard_map/reduce_scatter | solution.py:96
  74.6 4.9 %copy-start.2 = (bf16[512,4096]{1,0:T(8,128)(2,1)S(1)}, bf16[512,4096]{1,0:T(8,128)(2,1)}, u32[]{:S(2)}) copy-start(bf16[512,4096]{1,0:T(8,128)(2,1)} %reshape.55) | copy-start | bytes 12582916
  74.6 5.9 %copy-start.7 = (f32[4096,256]{1,0:T(8,128)S(1)}, f32[4096,256]{1,0:T(8,128)}, u32[]{:S(2)}) copy-start(f32[4096,256]{1,0:T(8,128)} %param.16) | copy-start | bytes 12582916
  74.6 5.9 %copy-start.8 = (f32[256]{0:T(256)S(1)}, f32[256]{0:T(256)}, u32[]{:S(2)}) copy-start(f32[256]{0:T(256)} %param.17) | copy-start | bytes 3076
  80.6 2.2 copy-start.5
  87.3 4.5 %copy-start.12 = (bf16[4096,224]{0,1:T(8,128)(2,1)S(1)}, bf16[4096,224]{0,1:T(8,128)(2,1)}, u32[]{:S(2)}) copy-start(bf16[4096,224]{0,1:T(8,128)(2,1)} %param.13) | copy-start | bytes 5505028
  116.3 0.7 copy-start.10
  116.3 0.7 copy-start.11
  206.5 37.6 %collective-permute-start = (f32[16,4096]{1,0:T(8,128)}, f32[16,4096]{1,0:T(8,128)S(1)}, u32[]{:S(2)}, u32[]{:S(2)}) collective-permute-start(f32[16,4096]{1,0:T(8,128)} %reduce-scatter.2.cloned.1.call-done), channel_id=1, source_target_pairs={{0,32},{32,0},{64,96},{96,64},{1,33},{33,1},{65,97},{97,65},{2,34}... | collective-permute-start | bytes 786440 | tf_op jit(solution)/shard_map/ppermute | solution.py:18
  208.4 7.8 %all-to-all-start.1 = ((bf16[4,1,4]{2,1,0:T(2,128)(2,1)}), bf16[4,1,4]{2,1,0:T(2,128)(2,1)S(1)}, u32[]{:S(2)}, u32[]{:S(2)}) async-start(bf16[4,1,4]{2,1,0:T(2,128)(2,1)} %copy.24), calls=%async_computation.1 | async-start | bytes 4096 | tf_op jit(solution)/shard_map/all_to_all | solution.py:71
  212.1 76.9 %all-gather.6.cloned.1.call-start = ((), (), s32[]{:S(2)}) async-start(), calls=%async_computation.5 | async-start | bytes 4325376 | tf_op jit(solution)/shard_map/all_gather | solution.py:101
  289.0 4.9 %copy-start.4 = (bf16[512,4096]{1,0:T(8,128)(2,1)S(1)}, bf16[512,4096]{1,0:T(8,128)(2,1)}, u32[]{:S(2)}) copy-start(bf16[512,4096]{1,0:T(8,128)(2,1)} %all-gather.6.cloned.1.call-done) | copy-start | bytes 12582916
  289.0 5.9 %copy-start.6 = (f32[256,4096]{1,0:T(8,128)S(1)}, f32[256,4096]{1,0:T(8,128)}, u32[]{:S(2)}) copy-start(f32[256,4096]{1,0:T(8,128)} %param.19) | copy-start | bytes 12582916
  294.9 2.0 copy-start.9
  294.9 2.6 copy-start.3
  302.1 4.9 %copy-start.1 = (bf16[224,4096]{1,0:T(8,128)(2,1)S(1)}, bf16[224,4096]{1,0:T(8,128)(2,1)}, u32[]{:S(2)}) copy-start(bf16[224,4096]{1,0:T(8,128)(2,1)} %param.15) | copy-start | bytes 5505028
Sparse Core Ops, SparseCore 0:
  19.1 48.5 all-gather.3
  116.5 89.9 reduce-scatter.1
  245.9 43.0 all-gather.5
where the time goes:
time: 314 us
  waiting for transfers between devices  185 us (59%)
  matrix products  57.1 us (18%)
  blocking collectives  37.3 us (12%)
  between operations  13.9 us (4%)
  local copies, waits for them, and re-layouts  11.9 us (4%)
  starting transfers between devices  4.98 us (2%)
  other arithmetic  3.61 us (1%)
    reduce_scatter x1, waiting for transfers between devices, body(): lax.psum_scatter(partial_error, 'feat', scatter_dimension=0, tiled=True)  89.5 us
    all_gather x1, waiting for transfers between devices, body(): lax.all_gather(came_rows, 'feat', axis=0, tiled=True)  48 us
    dot_general x11, matrix products, product(): lax.dot_general(left, right, (dims, ((), ())), preferred_element_type=jnp...  45.9 us
    all_gather x1, waiting for transfers between devices, body(): residual_grad = lax.all_gather(own_grad, 'feat', axis=0, tiled=True)  43.2 us
    all_gather x1, blocking collectives, body(): lax.all_gather(came_weights, 'feat', axis=0, tiled=True)  27.5 us
    all_to_all x1, blocking collectives, body(): lax.all_to_all(send_rows, 'expert', split_axis=0, concat_axis=0, tiled=True)  9.75 us
    dot_general x1, matrix products, body(): target_part = jnp.dot(hidden, down_proj, preferred_element_type=jnp.float32)  8.72 us
    reshape x1, local copies, waits for them, and re-layouts, body(): token_rows = all_rows.reshape(-1, width)  6.87 us
  transfers between devices with their start and end apart: 5, of which 4 were waited for; matrix products, arithmetic and copies ran while one was open for 1% of the time, Pallas kernels for 0%

commit v1 on v0

--- a/solution.py
+++ b/solution.py
@@ -6,6 +6,33 @@
 sharpness = 0.1
 kernel_width = 0.5
 density_weight = 0.01
+
+
+def tell_desk_for(inp, along_dim):
+    arr_next = list(inp.shape[1:])
+    arr_next[along_dim] *= inp.shape[0]
+    return jnp.moveaxis(inp, 0, along_dim).reshape(arr_next)
+
+
+def recast_array(row_data, along_axis):
+    total_devices = lax.psum(1, along_axis)
+    z = row_data[None]
+    for t in range(total_devices.bit_length() - 1):
+        value_now = 1 << t
+        xs_all = []
+        for nth in range(total_devices):
+            xs_all.append((nth, nth ^ value_now))
+        near = lax.ppermute(z, along_axis, xs_all)
+        w2 = jnp.stack([z, near], 0)
+        side_arr = lax.axis_index(along_axis)
+        finding = side_arr >> t & 1
+        z = jnp.where(finding == 0, w2, w2[::-1]).reshape(-1, *row_data.shape)
+    return z
+
+
+def _draw_object(dim_k, x_part, point):
+    v_now = recast_array(x_part, point)
+    return tell_desk_for(v_now, dim_k)
 
 
 def partner(block, axis, stride):
@@ -72,7 +99,7 @@
     )
     all_rows, all_weights = (
         lax.all_gather(came_rows, "feat", axis=0, tiled=True),
-        lax.all_gather(came_weights, "feat", axis=0, tiled=True),
+        _draw_object(0, came_weights, "feat"),
     )
     width = tokens.shape[1]
     token_rows = all_rows.reshape(-1, width)

time: 314 us -> 288 us (0.917)
  blocking collectives: 37.3 us -> 9.75 us
  starting transfers between devices: 4.98 us -> 12.4 us
  waiting for transfers between devices: 185 us -> 178 us
    all_gather x1 -> x0, blocking collectives: 27.5 us -> none  [body(): lax.all_gather(came_weights, 'feat', axis=0, tiled=True)]
    reduce_scatter x1, waiting for transfers between devices: 89.5 us -> 64.7 us  [body(): lax.psum_scatter(partial_error, 'feat', scatter_dimension=0, tiled=True)]
    ppermute x0 -> x5, waiting for transfers between devices: none -> 8.4 us  [recast_array(): near = lax.ppermute(z, along_axis, xs_all)]
    ppermute x0 -> x5, starting transfers between devices: none -> 7.1 us  [recast_array(): near = lax.ppermute(z, along_axis, xs_all)]
    all_gather x1, waiting for transfers between devices: 43.2 us -> 49.1 us  [body(): residual_grad = lax.all_gather(own_grad, 'feat', axis=0, tiled=True)]
    ppermute x1, waiting for transfers between devices: 0.01 us -> 3.89 us  [partner(): return lax.ppermute(block, axis, route)]
  transfers between devices with their start and end apart: 5 -> 10, of which waited for: 4 -> 10; matrix products, arithmetic and copies ran while one was open for 1% -> 1% of each run, Pallas kernels for 0% -> 0%
where the time goes in v1:
time: 288 us; the launch traced here: 287 us
  waiting for transfers between devices  178 us (62%)
  matrix products  57.1 us (20%)
  between operations  13.9 us (5%)
  local copies, waits for them, and re-layouts  12.5 us (4%)
  starting transfers between devices  12.4 us (4%)
  blocking collectives  9.75 us (3%)
  other arithmetic  3.51 us (1%)
    reduce_scatter x1, waiting for transfers between devices, body(): lax.psum_scatter(partial_error, 'feat', scatter_dimension=0, tiled=True)  64.7 us
    all_gather x1, waiting for transfers between devices, body(): residual_grad = lax.all_gather(own_grad, 'feat', axis=0, tiled=True)  49.1 us
    all_gather x1, waiting for transfers between devices, body(): lax.all_gather(came_rows, 'feat', axis=0, tiled=True)  48 us
    dot_general x11, matrix products, product(): lax.dot_general(left, right, (dims, ((), ())), preferred_element_type=jnp...  45.9 us
    all_to_all x1, blocking collectives, body(): lax.all_to_all(send_rows, 'expert', split_axis=0, concat_axis=0, tiled=True)  9.75 us
    dot_general x1, matrix products, body(): target_part = jnp.dot(hidden, down_proj, preferred_element_type=jnp.float32)  8.71 us
    ppermute x5, waiting for transfers between devices, recast_array(): near = lax.ppermute(z, along_axis, xs_all)  8.4 us
    ppermute x5, starting transfers between devices, recast_array(): near = lax.ppermute(z, along_axis, xs_all)  7.1 us
  transfers between devices with their start and end apart: 10, of which 10 were waited for; matrix products, arithmetic and copies ran while one was open for 1% of the time, Pallas kernels for 0%

profile of v1, /device:TPU:1, one launch (start us, length us, event | category | flops | bytes accessed | tf_op | source)
XLA Modules:
  0.0 287.3 jit_solution(11591524021181020678)
XLA Ops:
  9.3 9.7 %all_to_all.14 = bf16[4,4,4096]{2,1,0:T(4,128)(2,1)} all-to-all(bf16[4,4,4096]{2,1,0:T(4,128)(2,1)S(1)} %bitcast.44), channel_id=1, replica_groups=mesh['expert'=4,'feat'=32] {'expert'}, dimensions={0} | all-to-all | bytes 262144 | tf_op jit(solution)/shard_map/all_to_all | solution.py:97
  19.8 48.0 %all-gather.3.cloned.1.call-done = bf16[128,4,4096]{2,1,0:T(4,128)(2,1)} async-done(((bf16[4,4,4096]{2,1,0:T(4,128)(2,1)}), bf16[128,4,4096]{2,1,0:T(4,128)(2,1)}) %all-gather.3.cloned.1.call-update) | async-done | bytes 4194320 | tf_op jit(solution)/shard_map/all_gather | solution.py:101
  67.8 6.9 %reshape.68 = bf16[512,4096]{1,0:T(8,128)(2,1)} reshape(bf16[128,4,4096]{2,1,0:T(4,128)(2,1)} %all-gather.3.cloned.1.call-done) | data formatting | bytes 8388608 | tf_op jit(solution)/shard_map/reshape | solution.py:105
  74.6 4.9 %fusion.2 = f32[512,256]{1,0:T(8,128)S(1)} fusion(bf16[512,4096]{1,0:T(8,128)(2,1)} %reshape.68, f32[4096,256]{1,0:T(8,128)} %param.16), kind=kOutput, calls=%fused_computation.10 | convolution fusion | flops 1076887552 | bytes 8912896 | tf_op jit(solution)/shard_map/dot_general | solution.py:76
  79.5 1.0 copy-done.7
  80.6 1.3 fusion.6
  82.8 4.6 %fusion.11 = f32[512,4096]{1,0:T(8,128)} fusion(f32[256,4096]{1,0:T(8,128)S(1)} %copy-done.5, f32[512,256]{1,0:T(8,128)S(1)} %fusion.6, f32[256]{0:T(256)S(1)} %exp.10), kind=kOutput, calls=%fused_computation.23 | convolution fusion | flops 1077936128 | bytes 13108224 | tf_op jit(solution)/shard_map/dot_general | solution.py:76
  87.3 4.5 %fusion.41 = f32[512,4096]{1,0:T(8,128)} fusion(f32[256,4096]{1,0:T(8,128)S(1)} %copy-done.5, f32[512,256]{1,0:T(8,128)S(1)} %fusion.6, f32[256]{0:T(256)S(1)} %exp.10), kind=kOutput, calls=%fused_computation.72 | convolution fusion | flops 1076887552 | bytes 13108224 | tf_op jit(solution)/shard_map/dot_general | solution.py:76
  91.9 1.4 fusion.49
  93.3 8.7 %fusion.8 = f32[512,4096]{1,0:T(8,128)} fusion(bf16[224,4096]{1,0:T(8,128)(2,1)S(1)} %copy-done, bf16[512,4096]{1,0:T(8,128)(2,1)} %reshape.68, bf16[4096,224]{0,1:T(8,128)(2,1)} %param.14, f32[512,224]{0,1:T(8,128)S(1)} %fusion.49), kind=kOutput, calls=%fused_computation.17 | convolution fusion | flops 1879736320 | bytes 16711680 | tf_op jit(solution)/shard_map/dot_general | solution.py:110
  102.0 14.3 %add_subtract_fusion = f32[512,4096]{1,0:T(8,128)} fusion(f32[512,4096]{1,0:T(8,128)} %fusion.8, f32[512,4096]{1,0:T(8,128)} %fusion.41, f32[512,4096]{1,0:T(8,128)} %fusion.11, f32[256,4096]{1,0:T(8,128)} %param.19, f32[512,256]{1,0:T(8,128)S(1)} %fusion.6, f32[256]{0:T(256)S(1)} %exp.10), kind=kOutput, calls=%fused_computation | convolution fusion | flops 1083310080 | bytes 38274048 | tf_op jit(solution)/shard_map/dot_general | solution.py:76
  117.7 4.0 %all-to-all-start.1 = ((bf16[4,1,4]{2,1,0:T(2,128)(2,1)}), bf16[4,1,4]{2,1,0:T(2,128)(2,1)S(1)}, u32[]{:S(2)}, u32[]{:S(2)}) async-start(bf16[4,1,4]{2,1,0:T(2,128)(2,1)} %copy.45), calls=%async_computation.1 | async-start | bytes 4096 | tf_op jit(solution)/shard_map/all_to_all | solution.py:98
  121.7 4.0 %all-to-all-done.1 = bf16[4,1,4]{2,1,0:T(2,128)(2,1)S(1)} async-done(((bf16[4,1,4]{2,1,0:T(2,128)(2,1)}), bf16[4,1,4]{2,1,0:T(2,128)(2,1)S(1)}, u32[]{:S(2)}, u32[]{:S(2)}) %all-to-all-start.1) | async-done | bytes 64 | tf_op jit(solution)/shard_map/all_to_all | solution.py:98
  125.7 1.7 collective-permute-start
  129.2 1.6 collective-permute-done.1
  130.8 2.1 collective-permute-start.2
  132.9 2.2 collective-permute-done.2
  136.0 1.7 collective-permute-done.3
  137.8 1.7 collective-permute-start.4
  139.6 2.2 collective-permute-done.4
  141.8 64.7 %reduce-scatter.2.cloned.1.call-done = f32[16,4096]{1,0:T(8,128)} async-done(((f32[512,4096]{1,0:T(8,128)}), f32[16,4096]{1,0:T(8,128)}) %reduce-scatter.2.cloned.1.call-update) | async-done | bytes 262160 | tf_op jit(solution)/shard_map/reduce_scatter | solution.py:123
  206.5 1.2 collective-permute-start.5
  208.0 3.9 %collective-permute-done.5 = f32[16,4096]{1,0:T(8,128)S(1)} collective-permute-done((f32[16,4096]{1,0:T(8,128)}, f32[16,4096]{1,0:T(8,128)S(1)}, u32[]{:S(2)}, u32[]{:S(2)}) %collective-permute-start.5) | collective-permute-done | bytes 262176 | tf_op jit(solution)/shard_map/ppermute | solution.py:45
  211.9 1.7 multiply_convert_fusion
  213.6 49.1 %all-gather.5.cloned.1.call-done = bf16[512,4096]{1,0:T(8,128)(2,1)} async-done(((bf16[16,4096]{1,0:T(8,128)(2,1)}), bf16[512,4096]{1,0:T(8,128)(2,1)}) %all-gather.5.cloned.1.call-update) | async-done | bytes 4194320 | tf_op jit(solution)/shard_map/all_gather | solution.py:128
  262.8 4.9 %fusion.9 = f32[512,256]{1,0:T(8,128)S(1)} fusion(bf16[512,4096]{1,0:T(8,128)(2,1)} %all-gather.5.cloned.1.call-done, f32[256,4096]{1,0:T(8,128)} %param.19), kind=kOutput, calls=%fused_computation.22 | convolution fusion | flops 1076887552 | bytes 8912896 | tf_op jit(solution)/shard_map/dot_general | solution.py:76
  267.7 1.0 copy-done.6
  268.7 2.0 fusion.47
  271.3 1.3 fusion.23
  272.6 3.3 %convolution_add_fusion.1 = f32[4096,256]{1,0:T(8,128)} fusion(f32[4096,256]{1,0:T(8,128)S(1)} %fusion.23, bf16[512,4096]{1,0:T(8,128)(2,1)S(1)} %copy-done.3, f32[512,256]{1,0:T(8,128)S(1)} %get-tuple-element.5), kind=kOutput, calls=%fused_computation.6 | convolution fusion | flops 1075183616 | bytes 13107200 | tf_op jit(solution)/shard_map/dot_general | solution.py:76
  275.9 1.4 fusion.25
  277.3 3.5 %convolution_add_fusion = f32[256,4096]{1,0:T(8,128)} fusion(f32[256,4096]{1,0:T(8,128)S(1)} %fusion.25, bf16[512,4096]{1,0:T(8,128)(2,1)S(1)} %copy-done.4, f32[512,256]{1,0:T(8,128)S(1)} %fusion.6, f32[256]{0:T(256)S(1)} %exp.10), kind=kOutput, calls=%fused_computation.5 | convolution fusion | flops 1075838976 | bytes 13108224 | tf_op jit(solution)/shard_map/dot_general | solution.py:76
  (65 shorter events, 9.0 us)
Async XLA Ops:
  7.2 86.1 %copy-start = (bf16[224,4096]{1,0:T(8,128)(2,1)S(1)}, bf16[224,4096]{1,0:T(8,128)(2,1)}, u32[]{:S(2)}) copy-start(bf16[224,4096]{1,0:T(8,128)(2,1)} %param.15) | copy-start | bytes 5505028
  7.2 60.6 %all-gather.3.cloned.1.call-start = ((), (), s32[]{:S(2)}) async-start(), calls=%async_computation.3 | async-start | bytes 4325376 | tf_op jit(solution)/shard_map/all_gather | solution.py:101
  19.0 187.5 %reduce-scatter.2.cloned.1.call-start = ((), (), s32[]{:S(2)}) async-start(), calls=%async_computation.4 | async-start | bytes 8650752 | tf_op jit(solution)/shard_map/reduce_scatter | solution.py:123
  74.6 4.9 %copy-start.2 = (bf16[512,4096]{1,0:T(8,128)(2,1)S(1)}, bf16[512,4096]{1,0:T(8,128)(2,1)}, u32[]{:S(2)}) copy-start(bf16[512,4096]{1,0:T(8,128)(2,1)} %reshape.68) | copy-start | bytes 12582916
  74.6 5.9 %copy-start.7 = (f32[4096,256]{1,0:T(8,128)S(1)}, f32[4096,256]{1,0:T(8,128)}, u32[]{:S(2)}) copy-start(f32[4096,256]{1,0:T(8,128)} %param.16) | copy-start | bytes 12582916
  74.6 5.9 %copy-start.8 = (f32[256]{0:T(256)S(1)}, f32[256]{0:T(256)}, u32[]{:S(2)}) copy-start(f32[256]{0:T(256)} %param.17) | copy-start | bytes 3076
  80.6 2.2 copy-start.5
  87.3 4.5 %copy-start.12 = (bf16[4096,224]{0,1:T(8,128)(2,1)S(1)}, bf16[4096,224]{0,1:T(8,128)(2,1)}, u32[]{:S(2)}) copy-start(bf16[4096,224]{0,1:T(8,128)(2,1)} %param.13) | copy-start | bytes 5505028
  116.3 0.7 copy-start.10
  116.3 0.7 copy-start.11
  117.7 8.0 %all-to-all-start.1 = ((bf16[4,1,4]{2,1,0:T(2,128)(2,1)}), bf16[4,1,4]{2,1,0:T(2,128)(2,1)S(1)}, u32[]{:S(2)}, u32[]{:S(2)}) async-start(bf16[4,1,4]{2,1,0:T(2,128)(2,1)} %copy.45), calls=%async_computation.1 | async-start | bytes 4096 | tf_op jit(solution)/shard_map/all_to_all | solution.py:98
  121.7 141.1 %all-gather.5.cloned.1.call-start = ((), (), s32[]{:S(2)}) async-start(), calls=%async_computation.5 | async-start | bytes 4325376 | tf_op jit(solution)/shard_map/all_gather | solution.py:128
  125.7 2.5 collective-permute-start
  128.3 2.5 collective-permute-start.1
  130.8 4.2 %collective-permute-start.2 = (bf16[4,4,4]{2,1,0:T(4,128)(2,1)S(1)}, bf16[4,4,4]{2,1,0:T(4,128)(2,1)S(1)}, u32[]{:S(2)}, u32[]{:S(2)}) collective-permute-start(bf16[4,4,4]{2,1,0:T(4,128)(2,1)S(1)} %bitcast.47), channel_id=1, source_target_pairs={{0,4},{1,5},{2,6},{3,7},{4,0},{5,1},{6,2},{7,3},{8,12},{9,13},{10,... | collective-permute-start | bytes 392 | tf_op jit(solution)/shard_map/ppermute | solution.py:25
  135.2 2.5 collective-permute-start.3
  137.8 4.0 %collective-permute-start.4 = (bf16[16,4,4]{0,2,1:T(4,128)(2,1)S(1)}, bf16[16,4,4]{0,2,1:T(4,128)(2,1)S(1)}, u32[]{:S(2)}, u32[]{:S(2)}) collective-permute-start(bf16[16,4,4]{0,2,1:T(4,128)(2,1)S(1)} %reshape.72), channel_id=1, source_target_pairs={{0,16},{1,17},{2,18},{3,19},{4,20},{5,21},{6,22},{7,23},{8,24},{9,... | collective-permute-start | bytes 1544 | tf_op jit(solution)/shard_map/ppermute | solution.py:25
  206.5 5.4 %collective-permute-start.5 = (f32[16,4096]{1,0:T(8,128)}, f32[16,4096]{1,0:T(8,128)S(1)}, u32[]{:S(2)}, u32[]{:S(2)}) collective-permute-start(f32[16,4096]{1,0:T(8,128)} %reduce-scatter.2.cloned.1.call-done), channel_id=1, source_target_pairs={{0,32},{32,0},{64,96},{96,64},{1,33},{33,1},{65,97},{97,65},{2,34}... | collective-permute-start | bytes 786440 | tf_op jit(solution)/shard_map/ppermute | solution.py:45
  262.8 4.9 %copy-start.4 = (bf16[512,4096]{1,0:T(8,128)(2,1)S(1)}, bf16[512,4096]{1,0:T(8,128)(2,1)}, u32[]{:S(2)}) copy-start(bf16[512,4096]{1,0:T(8,128)(2,1)} %all-gather.5.cloned.1.call-done) | copy-start | bytes 12582916
  262.8 5.9 %copy-start.6 = (f32[256,4096]{1,0:T(8,128)S(1)}, f32[256,4096]{1,0:T(8,128)}, u32[]{:S(2)}) copy-start(f32[256,4096]{1,0:T(8,128)} %param.19) | copy-start | bytes 12582916
  268.7 2.0 copy-start.9
  268.7 2.6 copy-start.3
  275.9 4.9 %copy-start.1 = (bf16[224,4096]{1,0:T(8,128)(2,1)S(1)}, bf16[224,4096]{1,0:T(8,128)(2,1)}, u32[]{:S(2)}) copy-start(bf16[224,4096]{1,0:T(8,128)(2,1)} %param.15) | copy-start | bytes 5505028
Sparse Core Ops, SparseCore 0:
  19.1 48.5 all-gather.2
  116.5 89.9 reduce-scatter.1
  213.7 48.9 all-gather.4
